TPU v7x, 32 devices: a whole 2x2x4 slice. The times are simulated.
32 devices in a mesh: dp: 8 (over z, y), tensor: 4 (over x, core).
Axes of the slice: x: 2, y: 2, z: 4, core: 2. Of those that a mesh axis runs over, the one named last changes fastest.
Arguments:
- inputs: bfloat16 [32, 256, 1024], P('dp'), may hold values from -6 to 6
- cotangent: bfloat16 [32, 256, 1024], P('dp'), may hold values from -6 to 6
- lengths: int32 [32], P('dp'), may hold values from 1 to 256, as said below
- up_weight: bfloat16 [1024, 2048], P(None, 'tensor')
- down_weight: bfloat16 [2048, 1024], P('tensor')
- noise_up: float32 [1024, 2048], P(None, 'tensor'), may hold values from -16 to 16
- noise_down: float32 [2048, 1024], P('tensor'), may hold values from -16 to 16
Outputs:
- grad_up: float32 [1024, 2048], P(None, 'tensor')
- grad_down: float32 [2048, 1024], P('tensor')
- input_grad: bfloat16 [32, 256, 1024], P('dp', None, 'tensor')
Inputs may be any that keep to these rules, and one draw needn't show every extreme that they name: `lengths`: positions at or beyond a user's length are padding.
All inputs are finite; a program needn't handle non-finite values.
Results may differ from a plain program's by a relative error of at most 0.009.
Values may be sent and summed in bfloat16 or wider, within the bound.
A program may use at most 128 MiB of HBM per device.

v0:
```python
import jax
import jax.numpy as jnp
from jax import lax
from jax.sharding import PartitionSpec as P

D = 1024
FF = 2048


clip_scale = 0.25
norm_epsilon = 1e-06


def gelu_slope(pre, back):
    return jax.vjp(jax.nn.gelu, pre)[1](back)[0]


def per_device(inputs, cotangent, lengths, up_weight, down_weight, noise_up, noise_down):
    members = inputs.shape[0]
    clip_bound = jnp.float32(clip_scale * (D * FF) ** 0.5)
    positions = lax.broadcasted_iota(jnp.int32, (members, inputs.shape[1]), 1)
    mask = (positions < lengths[:, None])[:, :, None]
    masked = jnp.where(mask, cotangent, jnp.zeros_like(cotangent))
    pre = jnp.einsum("usd,df->usf", inputs, up_weight, preferred_element_type=jnp.float32)
    active = jax.nn.gelu(pre).astype(jnp.bfloat16)
    back = jnp.einsum("usd,fd->usf", masked, down_weight, preferred_element_type=jnp.float32)
    slopes = gelu_slope(pre, back).astype(jnp.bfloat16)
    token_terms = jnp.einsum("usf,df->usd", slopes, up_weight, preferred_element_type=jnp.float32)
    input_grad = lax.psum_scatter(
        token_terms.astype(jnp.bfloat16), "tensor", scatter_dimension=2, tiled=True
    )
    down_each = jnp.einsum("usf,usd->ufd", active, masked, preferred_element_type=jnp.float32)
    up_each = jnp.einsum("usd,usf->udf", inputs, slopes, preferred_element_type=jnp.float32)
    partial_sq = jnp.sum(down_each * down_each, axis=(1, 2)) + jnp.sum(
        up_each * up_each, axis=(1, 2)
    )
    squares = lax.psum(partial_sq, "tensor")
    factors = jnp.minimum(jnp.float32(1.0), clip_bound / jnp.sqrt(squares + norm_epsilon))
    sum_down = jnp.sum(factors[:, None, None] * down_each, axis=0)
    sum_up = jnp.sum(factors[:, None, None] * up_each, axis=0)
    total_up, total_down = lax.psum((sum_up, sum_down), "dp")
    grad_up = total_up + noise_up
    grad_down = total_down + noise_down
    return (grad_up, grad_down, input_grad)


def solution(mesh):
    placed = (
        P("dp", None, None),
        P("dp", None, None),
        P("dp"),
        P(None, "tensor"),
        P("tensor", None),
        P(None, "tensor"),
        P("tensor", None),
    )
    return jax.shard_map(
        per_device,
        mesh=mesh,
        in_specs=placed,
        out_specs=(P(None, "tensor"), P("tensor", None), P("dp", None, "tensor")),
        check_vma=False,
    )
```

profile of v0, /device:TPU:0, one launch (start us, length us, event | category | flops | bytes accessed | tf_op | source)
XLA Modules:
  0.0 218.4 jit_solution(308625782123852206)
XLA Ops:
  8.0 0.0 copy-start
  8.0 0.0 all-reduce.3.cloned.1.call-start
  8.1 0.9 iota_compare_fusion
  8.9 0.7 copy-done
  9.6 0.0 copy-start.1
  9.6 2.6 %fusion.11 = f32[4,256,512]{2,1,0:T(8,128)S(1)} fusion(bf16[4,256,1024]{2,1,0:T(8,128)(2,1)S(1)} %copy-done, bf16[1024,512]{1,0:T(8,128)(2,1)} %param.10), kind=kOutput, calls=%fused_computation.20 | convolution fusion | flops 1073741824 | bytes 5242880 | tf_op jit(solution)/shard_map/usd,df->usf/dot_general | solution.py:24
  12.2 0.0 copy-done.1
  12.2 0.0 copy-start.2
  12.2 4.4 %multiply_reduce_fusion.3 = (f32[4]{0:T(128)S(1)}, f32[4,512,1024]{2,1,0:T(8,128)}) fusion(bf16[4,256,1024]{2,1,0:T(8,128)(2,1)S(1)} %copy-done.1, pred[4,256]{1,0:T(4,128)(4,1)S(1)} %iota_compare_fusion, f32[4,256,512]{2,1,0:T(8,128)S(1)} %fusion.11), kind=kOutput, calls=%fused_computation.3 | convolution fusion | flops 1083703296 | bytes 12583952 | tf_op jit(solution)/shard_map/usf,usd->ufd/dot_general | solution.py:32
  16.6 0.0 copy-done.2
  16.6 2.6 %fusion.6 = bf16[4,256,512]{2,1,0:T(8,128)(2,1)S(1)} fusion(f32[4,256,512]{2,1,0:T(8,128)S(1)} %fusion.11, bf16[4,256,1024]{2,1,0:T(8,128)(2,1)S(1)} %copy-done.1, pred[4,256]{1,0:T(4,128)(4,1)S(1)} %iota_compare_fusion, bf16[512,1024]{1,0:T(8,128)(2,1)S(1)} %copy-done.2), kind=kOutput, calls=%fused_computation.12 | convolution fusion | flops 1085276160 | bytes 6292480 | tf_op jit(solution)/shard_map/usd,fd->usf/dot_general | solution.py:26
  19.3 4.5 %multiply_reduce_fusion.2 = (f32[4]{0:T(128)S(1)}, f32[4,512,1024]{2,1,0:T(8,128)}) fusion(bf16[4,256,512]{2,1,0:T(8,128)(2,1)S(1)} %fusion.6, bf16[4,256,1024]{2,1,0:T(8,128)(2,1)S(1)} %copy-done), kind=kOutput, calls=%fused_computation.2 | convolution fusion | flops 1077936128 | bytes 11534352 | tf_op jit(solution)/shard_map/usd,usf->udf/dot_general | solution.py:33
  23.8 8.3 %psum.21 = f32[4]{0:T(128)S(1)} all-reduce(f32[4]{0:T(128)S(1)} %add.31), channel_id=1, replica_groups=mesh['dp'=8,'tensor'=4] {'tensor'}, use_global_device_ids=true, to_apply=%region_2.3 | all-reduce | flops 4 | bytes 32 | tf_op jit(solution)/shard_map/psum | solution.py:37
  32.1 10.6 %multiply_reduce_fusion = (f32[512,1024]{1,0:T(8,128)}, f32[512,1024]{1,0:T(8,128)}) fusion(f32[4,512,1024]{2,1,0:T(8,128)} %get-tuple-element.11, f32[4]{0:T(128)S(1)} %multiply_minimum_fusion, f32[4,512,1024]{2,1,0:T(8,128)} %get-tuple-element.13), kind=kLoop, calls=%fused_computation | loop fusion | flops 7340032 | bytes 20971536 | tf_op jit(solution)/shard_map/reduce_sum | solution.py:39
  42.7 0.0 all-reduce.3.cloned.1.call-update
  42.8 0.0 reduce-scatter.2.cloned.1.call-start
  42.8 3.8 %convolution_convert_fusion = bf16[4,256,1024]{2,1,0:T(8,128)(2,1)} fusion(bf16[4,256,512]{2,1,0:T(8,128)(2,1)S(1)} %fusion.6, bf16[1024,512]{1,0:T(8,128)(2,1)} %param.10), kind=kOutput, calls=%fused_computation.15 | convolution fusion | flops 1074790400 | bytes 4194304 | tf_op jit(solution)/shard_map/usf,df->usd/dot_general | solution.py:28
  46.6 0.0 reduce-scatter.2.cloned.1.call-update
  46.6 2.9 %copy.14 = f32[1024,512]{0,1:T(8,128)} copy(f32[1024,512]{1,0:T(8,128)} %param.12) | data formatting | bytes 4194304 | tf_op args[5]
  49.6 150.3 %all-reduce.3.cloned.1.call-done = (f32[1024,512]{0,1:T(8,128)}, f32[512,1024]{1,0:T(8,128)}) async-done(((f32[1024,512]{0,1:T(8,128)}, f32[512,1024]{1,0:T(8,128)}), (f32[1024,512]{0,1:T(8,128)}, f32[512,1024]{1,0:T(8,128)})) %all-reduce.3.cloned.1.call-update) | async-done | bytes 4194320 | tf_op jit(solution)/shard_map/psum | solution.py:41
  199.9 4.1 %add.33 = f32[1024,512]{0,1:T(8,128)} add(f32[1024,512]{0,1:T(8,128)} %get-tuple-element.8, f32[1024,512]{0,1:T(8,128)} %copy.14) | non-fusion elementwise | flops 524288 | bytes 6291456 | tf_op jit(solution)/shard_map/add | solution.py:42
  204.0 2.9 %copy.15 = f32[1024,512]{1,0:T(8,128)} copy(f32[1024,512]{0,1:T(8,128)} %add.33) | data formatting | bytes 4194304
  206.9 4.1 %add.34 = f32[512,1024]{1,0:T(8,128)} add(f32[512,1024]{1,0:T(8,128)} %get-tuple-element.9, f32[512,1024]{1,0:T(8,128)} %param.13) | non-fusion elementwise | flops 524288 | bytes 6291456 | tf_op jit(solution)/shard_map/add | solution.py:43
  211.0 0.0 reduce-scatter.2.cloned.1.call-done
  (2 shorter events, 0.0 us)
Async XLA Ops:
  8.0 1.6 copy-start
  8.0 191.9 %all-reduce.3.cloned.1.call-start = ((), (), s32[]{:S(2)}) async-start(), calls=%async_computation.2 | async-start | bytes 8388608 | tf_op jit(solution)/shard_map/psum | solution.py:41
  9.6 2.6 %copy-start.1 = (bf16[4,256,1024]{2,1,0:T(8,128)(2,1)S(1)}, bf16[4,256,1024]{2,1,0:T(8,128)(2,1)}, u32[]{:S(2)}) copy-start(bf16[4,256,1024]{2,1,0:T(8,128)(2,1)} %param.8) | copy-start | bytes 6291460
  12.2 4.4 %copy-start.2 = (bf16[512,1024]{1,0:T(8,128)(2,1)S(1)}, bf16[512,1024]{1,0:T(8,128)(2,1)}, u32[]{:S(2)}) copy-start(bf16[512,1024]{1,0:T(8,128)(2,1)} %param.11) | copy-start | bytes 3145732
  42.8 168.2 %reduce-scatter.2.cloned.1.call-start = ((), (), s32[]{:S(2)}) async-start(), calls=%async_computation.1 | async-start | bytes 2621440 | tf_op jit(solution)/shard_map/reduce_scatter | solution.py:29
Sparse Core Ops, SparseCore 0:
  42.9 156.9 all-reduce.2
Sparse Core Ops, SparseCore 1:
  46.7 31.7 reduce-scatter.1
where the time goes:
time: 219 us; the launch traced here: 218 us
  waiting for transfers between devices  150 us (68%)
  other arithmetic  19.7 us (9%)
  matrix products  17.9 us (8%)
  between operations  15.5 us (7%)
  blocking collectives  8.31 us (4%)
  local copies, waits for them, and re-layouts  6.49 us (3%)
    psum x1, waiting for transfers between devices, per_device(): total_up, total_down = lax.psum((sum_up, sum_down), 'dp')  150 us
    reduce_sum x1, other arithmetic, per_device(): sum_down = jnp.sum(factors[:, None, None] * down_each, axis=0)  10.6 us
    psum x1, blocking collectives, per_device(): squares = lax.psum(partial_sq, 'tensor')  8.31 us
    unnamed x8, local copies, waits for them, and re-layouts  6.49 us
    dot_general x1, matrix products, per_device(): jnp.einsum('usd,usf->udf', inputs, slopes, preferred_element_type=jnp.flo...  4.53 us
    dot_general x1, matrix products, per_device(): jnp.einsum('usf,usd->ufd', active, masked, preferred_element_type=jnp.flo...  4.39 us
  transfers between devices with their start and end apart: 2, of which 1 were waited for; matrix products, arithmetic and copies ran while one was open for 8% of the time, Pallas kernels for 0%

commit v1 on v0

v1 whole, which is shorter than its diff:
```python
import functools

import jax
import jax.numpy as jnp
from jax import lax
from jax.experimental import pallas as pl
from jax.experimental.pallas import tpu as pltpu
from jax.sharding import PartitionSpec as P

clip_scale = 0.25
norm_epsilon = 1e-06
ROWS = 256
CHUNK_COLS = 512
GELU_C = 0.7978845608028654
GELU_A = 0.044715
MESH_IDS = pl.DeviceIdType.MESH
F32 = jnp.float32
BF16 = jnp.bfloat16


def dot(a, b, ca, cb):
    return lax.dot_general(a, b, (((ca,), (cb,)), ((), ())), preferred_element_type=F32)


def kernel(
    n_dp, n_tensor, bound,
    lengths, x_ref, c_ref, wu_ref, wd_ref,
    up_out, down_out, tok_out,
    masked, act, slopes, token, token_in, squares, acc, gathered, *rest,
):
    levels = n_dp.bit_length() - 1
    outgoing, incoming = rest[:levels], rest[levels : 2 * levels]
    (sq_send, sq_recv, tok_send, tok_recv, red_send, red_recv, gat_send, gat_recv,
     out_sem) = rest[2 * levels :]
    users, seq, d = x_ref.shape
    f = wu_ref.shape[1]
    own_cols = d // n_tensor
    n_up = d // ROWS
    down_split = d // CHUNK_COLS
    n_chunks = acc.shape[0]
    me_dp = lax.axis_index("dp")
    me_t = lax.axis_index("tensor")

    def peer(j):
        return lax.rem(me_t + j, n_tensor)

    def slot_from(j):
        return n_tensor - j - 1

    bits, partners, offsets, others = [], [], [0], []
    for k in range(levels):
        count = ROWS >> (k + 1)
        bit = lax.rem(me_dp // (1 << k), 2)
        bits.append(bit)
        partners.append(me_dp + (1 - 2 * bit) * (1 << k))
        offsets.append(offsets[-1] + bit * count)
        others.append(offsets[-2] + (1 - bit) * count)

    barrier = pltpu.get_barrier_semaphore()
    for j in range(1, n_tensor):
        pl.semaphore_signal(barrier, inc=1, device_id=(me_dp, peer(j)), device_id_type=MESH_IDS)
    for k in range(levels):
        pl.semaphore_signal(barrier, inc=1, device_id=(partners[k], me_t), device_id_type=MESH_IDS)

    def first(u, carry):
        tokens = x_ref[u]
        pos = lax.broadcasted_iota(jnp.int32, (seq, d), 0)
        grads = jnp.where(pos < lengths[u], c_ref[u].astype(F32), 0.0).astype(BF16)
        masked[u] = grads
        pre = dot(tokens, wu_ref[...], 1, 0)
        back = dot(grads, wd_ref[...], 1, 1)
        sq = pre * pre
        t = jnp.tanh(GELU_C * (pre + GELU_A * (sq * pre)))
        half = 0.5 * (1.0 + t)
        a = (pre * half).astype(BF16)
        slope = half + 0.5 * pre * (1.0 - t * t) * (GELU_C * (1.0 + 3.0 * GELU_A * sq))
        s = (back * slope).astype(BF16)
        act[u] = a
        slopes[u] = s
        terms = dot(tokens, tokens, 1, 1) * dot(s, s, 1, 1)
        terms += dot(grads, grads, 1, 1) * dot(a, a, 1, 1)
        total = jnp.sum(jnp.sum(terms, axis=0, keepdims=True), axis=1, keepdims=True)
        squares[0, u] = jnp.broadcast_to(total, (8, 128))
        return carry

    lax.fori_loop(0, users, first, 0)

    pl.semaphore_wait(barrier, n_tensor - 1 + levels)

    def square_copy(j):
        return pltpu.make_async_remote_copy(
            src_ref=squares.at[0], dst_ref=squares.at[j],
            send_sem=sq_send.at[j - 1], recv_sem=sq_recv.at[j - 1],
            device_id=(me_dp, peer(j)), device_id_type=MESH_IDS,
        )

    for j in range(1, n_tensor):
        square_copy(j).start()

    def token_terms(u, carry):
        t = dot(slopes[u], wu_ref[...], 1, 1).astype(BF16)
        for k in range(n_tensor):
            token[k, u] = t[:, k * own_cols : (k + 1) * own_cols]
        return carry

    lax.fori_loop(0, users, token_terms, 0)

    def token_copy(j):
        return pltpu.make_async_remote_copy(
            src_ref=token.at[peer(j)], dst_ref=token_in.at[j - 1],
            send_sem=tok_send.at[j - 1], recv_sem=tok_recv.at[j - 1],
            device_id=(me_dp, peer(j)), device_id_type=MESH_IDS,
        )

    for j in range(1, n_tensor):
        token_copy(j).start()

    for j in range(1, n_tensor):
        square_copy(j).wait()
    total_sq = squares[0]
    for j in range(1, n_tensor):
        total_sq += squares[j]
    factors = jnp.minimum(1.0, bound / jnp.sqrt(jnp.maximum(total_sq, 0.0) + norm_epsilon))
    scale = [factors[u, 0:1, 0:1] for u in range(users)]

    def reduce_copy(c, k):
        return pltpu.make_async_remote_copy(
            src_ref=outgoing[k].at[c], dst_ref=incoming[k].at[c],
            send_sem=red_send.at[k, c], recv_sem=red_recv.at[k, c],
            device_id=(partners[k], me_t), device_id_type=MESH_IDS,
        )

    def gather_copy(c, k):
        count = ROWS >> (k + 1)
        rows = pl.ds(pl.multiple_of(offsets[k + 1], count), count)
        return pltpu.make_async_remote_copy(
            src_ref=gathered.at[c, rows], dst_ref=gathered.at[c, rows],
            send_sem=gat_send.at[k, c], recv_sem=gat_recv.at[k, c],
            device_id=(partners[k], me_t), device_id_type=MESH_IDS,
        )

    def send_half(c, k):
        count = ROWS >> (k + 1)
        outgoing[k][c] = acc[c, pl.ds(pl.multiple_of(others[k], count), count)].astype(BF16)
        reduce_copy(c, k).start()

    def up_chunk(i, carry):
        cols = pl.ds(pl.multiple_of(i * ROWS, ROWS), ROWS)
        value = scale[0] * dot(x_ref[0, :, cols], slopes[0], 0, 0)
        for u in range(1, users):
            value += scale[u] * dot(x_ref[u, :, cols], slopes[u], 0, 0)
        acc[i] = value
        send_half(i, 0)
        return carry

    def down_chunk(i, carry):
        rows = pl.ds(pl.multiple_of((i // down_split) * ROWS, ROWS), ROWS)
        cols = pl.ds(pl.multiple_of((i % down_split) * CHUNK_COLS, CHUNK_COLS), CHUNK_COLS)
        value = scale[0] * dot(act[0, :, rows], masked[0, :, cols], 0, 0)
        for u in range(1, users):
            value += scale[u] * dot(act[u, :, rows], masked[u, :, cols], 0, 0)
        acc[n_up + i] = value
        send_half(n_up + i, 0)
        return carry

    lax.fori_loop(0, n_up, up_chunk, 0)
    lax.fori_loop(0, n_chunks - n_up, down_chunk, 0)

    def up_copy(c):
        return pltpu.make_async_copy(
            gathered.at[c], up_out.at[pl.ds(pl.multiple_of(c * ROWS, ROWS), ROWS)], out_sem.at[c]
        )

    def down_copy(c):
        i = c - n_up
        rows = pl.ds(pl.multiple_of((i // down_split) * ROWS, ROWS), ROWS)
        cols = pl.ds(pl.multiple_of((i % down_split) * CHUNK_COLS, CHUNK_COLS), CHUNK_COLS)
        return pltpu.make_async_copy(gathered.at[c], down_out.at[rows, cols], out_sem.at[c])

    def stage(c, s):
        if s < levels:
            k = s
            count = ROWS >> (k + 1)
            mine = pl.ds(pl.multiple_of(offsets[k + 1], count), count)
            reduce_copy(c, k).wait()
            acc[c, mine] += incoming[k][c].astype(F32)
            if k + 1 < levels:
                send_half(c, k + 1)
            else:
                gathered[c, mine] = acc[c, mine].astype(BF16)
                gather_copy(c, k).start()
        else:
            k = 2 * levels - 1 - s
            gather_copy(c, k).wait()
            if k > 0:
                gather_copy(c, k - 1).start()
            else:
                @pl.when(c < n_up)
                def _():
                    up_copy(c).start()

                @pl.when(c >= n_up)
                def _():
                    down_copy(c).start()

    def slot(t, carry):
        for s in reversed(range(2 * levels)):
            @pl.when((t >= s) & (t - s < n_chunks))
            def _():
                stage(t - s, s)
        return carry

    lax.fori_loop(0, n_chunks + 2 * levels - 1, slot, 0)

    for j in range(1, n_tensor):
        token_copy(j).wait()

    def finish(u, carry):
        total = token[me_t, u].astype(F32)
        for j in range(1, n_tensor):
            total += token_in[j - 1, u].astype(F32)
        tok_out[u] = total.astype(BF16)
        return carry

    lax.fori_loop(0, users, finish, 0)

    lax.fori_loop(0, n_up, lambda c, carry: (up_copy(c).wait(), carry)[1], 0)
    lax.fori_loop(n_up, n_chunks, lambda c, carry: (down_copy(c).wait(), carry)[1], 0)


def fused(n_dp, n_tensor, inputs, cotangent, lengths, up_weight, down_weight, noise_up, noise_down):
    users, seq, d = inputs.shape
    f = up_weight.shape[1]
    bound = clip_scale * (d * f * n_tensor) ** 0.5
    levels = n_dp.bit_length() - 1
    n_chunks = d // ROWS + (f // ROWS) * (d // CHUNK_COLS)
    own = d // n_tensor
    vmem = pl.BlockSpec(memory_space=pltpu.VMEM)
    smem = pl.BlockSpec(memory_space=pltpu.SMEM)
    anyspace = pl.BlockSpec(memory_space=pl.ANY)
    halves = [pltpu.VMEM((n_chunks, ROWS >> (k + 1), CHUNK_COLS), BF16) for k in range(levels)]
    sem = pltpu.SemaphoreType.DMA
    total_up, total_down, input_grad = pl.pallas_call(
        functools.partial(kernel, n_dp, n_tensor, bound),
        out_shape=(
            jax.ShapeDtypeStruct((d, f), BF16),
            jax.ShapeDtypeStruct((f, d), BF16),
            jax.ShapeDtypeStruct((users, seq, own), BF16),
        ),
        in_specs=[smem, vmem, vmem, vmem, vmem],
        out_specs=(anyspace, anyspace, vmem),
        scratch_shapes=[
            pltpu.VMEM((users, seq, d), BF16),
            pltpu.VMEM((users, seq, f), BF16),
            pltpu.VMEM((users, seq, f), BF16),
            pltpu.VMEM((n_tensor, users, seq, own), BF16),
            pltpu.VMEM((n_tensor - 1, users, seq, own), BF16),
            pltpu.VMEM((n_tensor, users, 8, 128), F32),
            pltpu.VMEM((n_chunks, ROWS, CHUNK_COLS), F32),
            pltpu.VMEM((n_chunks, ROWS, CHUNK_COLS), BF16),
            *halves,
            *halves,
            sem((n_tensor - 1,)), sem((n_tensor - 1,)),
            sem((n_tensor - 1,)), sem((n_tensor - 1,)),
            sem((levels, n_chunks)), sem((levels, n_chunks)),
            sem((levels, n_chunks)), sem((levels, n_chunks)),
            sem((n_chunks,)),
        ],
        compiler_params=pltpu.CompilerParams(
            collective_id=0, has_side_effects=True, vmem_limit_bytes=48 * 1024 * 1024
        ),
    )(lengths, inputs, cotangent, up_weight, down_weight)
    return (
        total_up.astype(F32) + noise_up,
        total_down.astype(F32) + noise_down,
        input_grad,
    )


def gelu_slope(pre, back):
    return jax.vjp(jax.nn.gelu, pre)[1](back)[0]


def plain(n_tensor, inputs, cotangent, lengths, up_weight, down_weight, noise_up, noise_down):
    members, seq, d = inputs.shape
    bound = F32(clip_scale * (d * up_weight.shape[1] * n_tensor) ** 0.5)
    positions = lax.broadcasted_iota(jnp.int32, (members, seq), 1)
    mask = (positions < lengths[:, None])[:, :, None]
    masked = jnp.where(mask, cotangent, jnp.zeros_like(cotangent))
    pre = jnp.einsum("usd,df->usf", inputs, up_weight, preferred_element_type=F32)
    active = jax.nn.gelu(pre).astype(BF16)
    back = jnp.einsum("usd,fd->usf", masked, down_weight, preferred_element_type=F32)
    slopes = gelu_slope(pre, back).astype(BF16)
    token_terms = jnp.einsum("usf,df->usd", slopes, up_weight, preferred_element_type=F32)
    input_grad = lax.psum_scatter(
        token_terms.astype(BF16), "tensor", scatter_dimension=2, tiled=True
    )
    down_each = jnp.einsum("usf,usd->ufd", active, masked, preferred_element_type=F32)
    up_each = jnp.einsum("usd,usf->udf", inputs, slopes, preferred_element_type=F32)
    partial_sq = jnp.sum(down_each * down_each, axis=(1, 2)) + jnp.sum(
        up_each * up_each, axis=(1, 2)
    )
    squares = lax.psum(partial_sq, "tensor")
    factors = jnp.minimum(F32(1.0), bound / jnp.sqrt(squares + norm_epsilon))
    sum_down = jnp.sum(factors[:, None, None] * down_each, axis=0)
    sum_up = jnp.sum(factors[:, None, None] * up_each, axis=0)
    total_up, total_down = lax.psum((sum_up, sum_down), "dp")
    return (total_up + noise_up, total_down + noise_down, input_grad)


def solution(mesh):
    n_dp, n_tensor = mesh.shape["dp"], mesh.shape["tensor"]

    def per_device(*args):
        d, f = args[3].shape
        fits = n_dp & (n_dp - 1) == 0 and 2 <= n_dp <= ROWS // 16 and n_tensor > 1
        fits = fits and f == CHUNK_COLS and d % CHUNK_COLS == 0 and (d // n_tensor) % 128 == 0
        if fits:
            return fused(n_dp, n_tensor, *args)
        return plain(n_tensor, *args)

    placed = (
        P("dp", None, None),
        P("dp", None, None),
        P("dp"),
        P(None, "tensor"),
        P("tensor", None),
        P(None, "tensor"),
        P("tensor", None),
    )
    return jax.shard_map(
        per_device,
        mesh=mesh,
        in_specs=placed,
        out_specs=(P(None, "tensor"), P("tensor", None), P("dp", None, "tensor")),
        check_vma=False,
    )
```

time: 219 us -> 85.4 us (0.39)
  waiting for transfers between devices: 150 us -> 0 us
  Pallas kernels: 0 us -> 76.7 us
  matrix products: 17.9 us -> 0 us
  other arithmetic: 19.7 us -> 3.31 us
  between operations: 15.5 us -> 0.67 us
  blocking collectives: 8.31 us -> 0 us
    psum x1 -> x0, waiting for transfers between devices: 150 us -> none  [per_device(): total_up, total_down = lax.psum((sum_up, sum_down), 'dp')]
    pallas_call x0 -> x1, Pallas kernels: none -> 76.7 us  [fused(): pl.pallas_call(functools.partial(kernel, n_dp, n_tensor, bound), out_shap...]
    dot_general x5 -> x0, matrix products: 17.9 us -> none  [the longest x1 4.53 us: per_device(): jnp.einsum('usd,usf->udf', inputs, slopes, preferred_element_type=jnp.flo...]
    reduce_sum x1 -> x0, other arithmetic: 10.6 us -> none  [per_device(): sum_down = jnp.sum(factors[:, None, None] * down_each, axis=0)]
    psum x1 -> x0, blocking collectives: 8.31 us -> none  [per_device(): squares = lax.psum(partial_sq, 'tensor')]
    add x3 -> x2, other arithmetic: 8.2 us -> 3.31 us  [the longest x1 1.66 us: fused(): total_up.astype(F32) + noise_up]
    unnamed x8 -> x11, local copies, waits for them, and re-layouts: 6.49 us -> 4.48 us
  transfers between devices with their start and end apart: 2 -> 0, of which waited for: 1 -> 0; matrix products, arithmetic and copies ran while one was open for 8% -> 0% of each run, Pallas kernels for 0% -> 0%
where the time goes in v1:
time: 85.4 us; the launch traced here: 85.2 us
  Pallas kernels  76.7 us (90%)
  local copies, waits for them, and re-layouts  4.48 us (5%)
  other arithmetic  3.31 us (4%)
    pallas_call x1, Pallas kernels, fused(): pl.pallas_call(functools.partial(kernel, n_dp, n_tensor, bound), out_shap...  76.7 us
    unnamed x11, local copies, waits for them, and re-layouts  4.48 us

profile of v1, /device:TPU:0, one launch (start us, length us, event | category | flops | bytes accessed | tf_op | source)
XLA Modules:
  0.0 85.2 jit_solution(370052790464131921)
XLA Ops:
  0.6 0.0 copy-start
  0.6 1.2 %copy-done = bf16[1024,512]{1,0:T(8,128)(2,1)S(1)} copy-done((bf16[1024,512]{1,0:T(8,128)(2,1)S(1)}, bf16[1024,512]{1,0:T(8,128)(2,1)}, u32[]{:S(2)}) %copy-start) | copy-done | bytes 1048600
  1.9 0.0 copy-start.1
  1.9 1.2 %copy-done.1 = bf16[512,1024]{1,0:T(8,128)(2,1)S(1)} copy-done((bf16[512,1024]{1,0:T(8,128)(2,1)S(1)}, bf16[512,1024]{1,0:T(8,128)(2,1)}, u32[]{:S(2)}) %copy-start.1) | copy-done | bytes 1048600
  3.1 0.0 copy-start.2
  3.1 0.7 copy-done.2
  3.7 0.0 copy-start.3
  3.7 76.7 %shard_map.94 = (bf16[1024,512]{1,0:T(8,128)(2,1)S(1)}, bf16[512,1024]{1,0:T(8,128)(2,1)S(1)}, bf16[4,256,256]{2,1,0:T(8,128)(2,1)S(1)}) custom-call(s32[4]{0:T(128)S(1)} %copy-done.2, bf16[4,256,1024]{2,1,0:T(8,128)(2,1)} %x_ref.1, bf16[4,256,1024]{2,1,0:T(8,128)(2,1)} %c_ref.1, bf16[1024,512]{1,0:T(8,128)(2,1)S(1)} %copy-done, bf16[512,1024]{1,0:T(8,128)(2,1)S(1)} %copy-done.1), custom_call_target="tpu_custom_call" | custom-call | tf_op jit(solution)/shard_map/pallas_call | solution.py:243
  80.5 0.0 copy-done.3
  80.5 0.0 copy-start.4
  80.5 1.7 %convert_add_fusion.1 = f32[1024,512]{1,0:T(8,128)} fusion(f32[1024,512]{1,0:T(8,128)S(1)} %copy-done.3, bf16[1024,512]{1,0:T(8,128)(2,1)S(1)} %get-tuple-element.6), kind=kLoop, calls=%fused_computation.1 | loop fusion | flops 1048576 | bytes 5242880 | tf_op jit(solution)/shard_map/add | solution.py:274
  82.1 0.6 copy-done.4
  82.7 1.7 %convert_add_fusion = f32[512,1024]{1,0:T(8,128)} fusion(f32[512,1024]{1,0:T(8,128)S(1)} %copy-done.4, bf16[512,1024]{1,0:T(8,128)(2,1)S(1)} %get-tuple-element.7), kind=kLoop, calls=%fused_computation | loop fusion | flops 1048576 | bytes 5242880 | tf_op jit(solution)/shard_map/add | solution.py:275
  84.4 0.8 copy.11
Async XLA Ops:
  0.6 1.2 %copy-start = (bf16[1024,512]{1,0:T(8,128)(2,1)S(1)}, bf16[1024,512]{1,0:T(8,128)(2,1)}, u32[]{:S(2)}) copy-start(bf16[1024,512]{1,0:T(8,128)(2,1)} %wu_ref.1) | copy-start | bytes 3145732
  1.9 1.2 %copy-start.1 = (bf16[512,1024]{1,0:T(8,128)(2,1)S(1)}, bf16[512,1024]{1,0:T(8,128)(2,1)}, u32[]{:S(2)}) copy-start(bf16[512,1024]{1,0:T(8,128)(2,1)} %wd_ref.1) | copy-start | bytes 3145732
  3.1 0.7 copy-start.2
  3.7 76.7 %copy-start.3 = (f32[1024,512]{1,0:T(8,128)S(1)}, f32[1024,512]{1,0:T(8,128)}, u32[]{:S(2)}) copy-start(f32[1024,512]{1,0:T(8,128)} %param.12) | copy-start | bytes 6291460
  80.5 2.3 %copy-start.4 = (f32[512,1024]{1,0:T(8,128)S(1)}, f32[512,1024]{1,0:T(8,128)}, u32[]{:S(2)}) copy-start(f32[512,1024]{1,0:T(8,128)} %param.13) | copy-start | bytes 6291460

commit v2 on v1

--- a/solution.py
+++ b/solution.py
@@ -11,6 +11,7 @@
 norm_epsilon = 1e-06
 ROWS = 256
 CHUNK_COLS = 512
+AHEAD = 1
 GELU_C = 0.7978845608028654
 GELU_A = 0.044715
 MESH_IDS = pl.DeviceIdType.MESH
@@ -47,20 +48,20 @@
     def slot_from(j):
         return n_tensor - j - 1
 
-    bits, partners, offsets, others = [], [], [0], []
+    bits = [lax.rem(me_dp // (1 << k), 2) for k in range(levels)]
+    across = [me_dp + (1 - 2 * bits[k]) * (1 << k) for k in range(levels)]
+    offsets, others = [0], []
     for k in range(levels):
         count = ROWS >> (k + 1)
-        bit = lax.rem(me_dp // (1 << k), 2)
-        bits.append(bit)
-        partners.append(me_dp + (1 - 2 * bit) * (1 << k))
-        offsets.append(offsets[-1] + bit * count)
-        others.append(offsets[-2] + (1 - bit) * count)
+        others.append(offsets[-1] + (1 - bits[k]) * count)
+        offsets.append(offsets[-1] + bits[k] * count)
+    plan = (across, offsets, others)
 
     barrier = pltpu.get_barrier_semaphore()
     for j in range(1, n_tensor):
         pl.semaphore_signal(barrier, inc=1, device_id=(me_dp, peer(j)), device_id_type=MESH_IDS)
     for k in range(levels):
-        pl.semaphore_signal(barrier, inc=1, device_id=(partners[k], me_t), device_id_type=MESH_IDS)
+        pl.semaphore_signal(barrier, inc=1, device_id=(across[k], me_t), device_id_type=MESH_IDS)
 
     def first(u, carry):
         tokens = x_ref[u]
@@ -123,48 +124,52 @@
     factors = jnp.minimum(1.0, bound / jnp.sqrt(jnp.maximum(total_sq, 0.0) + norm_epsilon))
     scale = [factors[u, 0:1, 0:1] for u in range(users)]
 
-    def reduce_copy(c, k):
+    def reduce_copy(plan, c, k):
         return pltpu.make_async_remote_copy(
             src_ref=outgoing[k].at[c], dst_ref=incoming[k].at[c],
             send_sem=red_send.at[k, c], recv_sem=red_recv.at[k, c],
-            device_id=(partners[k], me_t), device_id_type=MESH_IDS,
-        )
-
-    def gather_copy(c, k):
+            device_id=(plan[0][k], me_t), device_id_type=MESH_IDS,
+        )
+
+    def gather_copy(plan, c, k):
         count = ROWS >> (k + 1)
-        rows = pl.ds(pl.multiple_of(offsets[k + 1], count), count)
+        rows = pl.ds(pl.multiple_of(plan[1][k + 1], count), count)
         return pltpu.make_async_remote_copy(
             src_ref=gathered.at[c, rows], dst_ref=gathered.at[c, rows],
             send_sem=gat_send.at[k, c], recv_sem=gat_recv.at[k, c],
-            device_id=(partners[k], me_t), device_id_type=MESH_IDS,
-        )
-
-    def send_half(c, k):
+            device_id=(plan[0][k], me_t), device_id_type=MESH_IDS,
+        )
+
+    def send_half(plan, c, k):
         count = ROWS >> (k + 1)
-        outgoing[k][c] = acc[c, pl.ds(pl.multiple_of(others[k], count), count)].astype(BF16)
-        reduce_copy(c, k).start()
-
-    def up_chunk(i, carry):
+        outgoing[k][c] = acc[c, pl.ds(pl.multiple_of(plan[2][k], count), count)].astype(BF16)
+        reduce_copy(plan, c, k).start()
+
+    def up_chunk(i):
         cols = pl.ds(pl.multiple_of(i * ROWS, ROWS), ROWS)
         value = scale[0] * dot(x_ref[0, :, cols], slopes[0], 0, 0)
         for u in range(1, users):
             value += scale[u] * dot(x_ref[u, :, cols], slopes[u], 0, 0)
         acc[i] = value
-        send_half(i, 0)
-        return carry
-
-    def down_chunk(i, carry):
+        send_half(plan, i, 0)
+
+    def down_chunk(i):
         rows = pl.ds(pl.multiple_of((i // down_split) * ROWS, ROWS), ROWS)
         cols = pl.ds(pl.multiple_of((i % down_split) * CHUNK_COLS, CHUNK_COLS), CHUNK_COLS)
         value = scale[0] * dot(act[0, :, rows], masked[0, :, cols], 0, 0)
         for u in range(1, users):
             value += scale[u] * dot(act[u, :, rows], masked[u, :, cols], 0, 0)
         acc[n_up + i] = value
-        send_half(n_up + i, 0)
-        return carry
-
-    lax.fori_loop(0, n_up, up_chunk, 0)
-    lax.fori_loop(0, n_chunks - n_up, down_chunk, 0)
+        send_half(plan, n_up + i, 0)
+
+    def produce(c):
+        @pl.when(c < n_up)
+        def _():
+            up_chunk(c)
+
+        @pl.when(c >= n_up)
+        def _():
+            down_chunk(c - n_up)
 
     def up_copy(c):
         return pltpu.make_async_copy(
@@ -177,40 +182,58 @@
         cols = pl.ds(pl.multiple_of((i % down_split) * CHUNK_COLS, CHUNK_COLS), CHUNK_COLS)
         return pltpu.make_async_copy(gathered.at[c], down_out.at[rows, cols], out_sem.at[c])
 
-    def stage(c, s):
+    def stage(plan, c, s):
         if s < levels:
             k = s
             count = ROWS >> (k + 1)
-            mine = pl.ds(pl.multiple_of(offsets[k + 1], count), count)
-            reduce_copy(c, k).wait()
+            mine = pl.ds(pl.multiple_of(plan[1][k + 1], count), count)
+            reduce_copy(plan, c, k).wait()
             acc[c, mine] += incoming[k][c].astype(F32)
             if k + 1 < levels:
-                send_half(c, k + 1)
+                send_half(plan, c, k + 1)
             else:
                 gathered[c, mine] = acc[c, mine].astype(BF16)
-                gather_copy(c, k).start()
+                gather_copy(plan, c, k).start()
         else:
             k = 2 * levels - 1 - s
-            gather_copy(c, k).wait()
+            gather_copy(plan, c, k).wait()
             if k > 0:
-                gather_copy(c, k - 1).start()
-            else:
-                @pl.when(c < n_up)
-                def _():
-                    up_copy(c).start()
-
-                @pl.when(c >= n_up)
-                def _():
-                    down_copy(c).start()
+                gather_copy(plan, c, k - 1).start()
+
+    def copy_out(c, wait):
+        @pl.when(c < n_up)
+        def _():
+            copy = up_copy(c)
+            copy.wait() if wait else copy.start()
+
+        @pl.when(c >= n_up)
+        def _():
+            copy = down_copy(c)
+            copy.wait() if wait else copy.start()
+
+    def prime(c, carry):
+        produce(c)
+        return carry
+
+    lax.fori_loop(0, AHEAD, prime, 0)
 
     def slot(t, carry):
-        for s in reversed(range(2 * levels)):
+        @pl.when(t + AHEAD < n_chunks)
+        def _():
+            produce(t + AHEAD)
+
+        for s in reversed(range(2 * levels - 1)):
             @pl.when((t >= s) & (t - s < n_chunks))
             def _():
-                stage(t - s, s)
-        return carry
-
-    lax.fori_loop(0, n_chunks + 2 * levels - 1, slot, 0)
+                stage(plan, t - s, s)
+        return carry
+
+    lax.fori_loop(0, n_chunks + 2 * levels - 2, slot, 0)
+
+    def last(c, carry):
+        stage(plan, c, 2 * levels - 1)
+        copy_out(c, False)
+        return carry
 
     for j in range(1, n_tensor):
         token_copy(j).wait()
@@ -223,9 +246,13 @@
         return carry
 
     lax.fori_loop(0, users, finish, 0)
-
-    lax.fori_loop(0, n_up, lambda c, carry: (up_copy(c).wait(), carry)[1], 0)
-    lax.fori_loop(n_up, n_chunks, lambda c, carry: (down_copy(c).wait(), carry)[1], 0)
+    lax.fori_loop(0, n_chunks, last, 0)
+
+    def drain(c, carry):
+        copy_out(c, True)
+        return carry
+
+    lax.fori_loop(0, n_chunks, drain, 0)
 
 
 def fused(n_dp, n_tensor, inputs, cotangent, lengths, up_weight, down_weight, noise_up, noise_down):

time: 85.4 us -> 81.1 us (0.950)
  Pallas kernels: 76.7 us -> 72.4 us
    pallas_call x1, Pallas kernels: 76.7 us -> 72.4 us  [fused(): pl.pallas_call(functools.partial(kernel, n_dp, n_tensor, bound), out_shap...]
where the time goes in v2:
time: 81.1 us; the launch traced here: 80.9 us
  Pallas kernels  72.4 us (89%)
  local copies, waits for them, and re-layouts  4.48 us (6%)
  other arithmetic  3.31 us (4%)
    pallas_call x1, Pallas kernels, fused(): pl.pallas_call(functools.partial(kernel, n_dp, n_tensor, bound), out_shap...  72.4 us
    unnamed x11, local copies, waits for them, and re-layouts  4.48 us
    add x1, other arithmetic, fused(): total_up.astype(F32) + noise_up  1.66 us
    add x1, other arithmetic, fused(): total_down.astype(F32) + noise_down  1.66 us

profile of v2, /device:TPU:0, one launch (start us, length us, event | category | flops | bytes accessed | tf_op | source)
XLA Modules:
  0.0 80.9 jit_solution(115048683108330948)
XLA Ops:
  0.6 0.0 copy-start
  0.6 1.2 %copy-done = bf16[1024,512]{1,0:T(8,128)(2,1)S(1)} copy-done((bf16[1024,512]{1,0:T(8,128)(2,1)S(1)}, bf16[1024,512]{1,0:T(8,128)(2,1)}, u32[]{:S(2)}) %copy-start) | copy-done | bytes 1048600
  1.9 0.0 copy-start.1
  1.9 1.2 %copy-done.1 = bf16[512,1024]{1,0:T(8,128)(2,1)S(1)} copy-done((bf16[512,1024]{1,0:T(8,128)(2,1)S(1)}, bf16[512,1024]{1,0:T(8,128)(2,1)}, u32[]{:S(2)}) %copy-start.1) | copy-done | bytes 1048600
  3.1 0.0 copy-start.2
  3.1 0.7 copy-done.2
  3.7 0.0 copy-start.3
  3.7 72.4 %shard_map.94 = (bf16[1024,512]{1,0:T(8,128)(2,1)S(1)}, bf16[512,1024]{1,0:T(8,128)(2,1)S(1)}, bf16[4,256,256]{2,1,0:T(8,128)(2,1)S(1)}) custom-call(s32[4]{0:T(128)S(1)} %copy-done.2, bf16[4,256,1024]{2,1,0:T(8,128)(2,1)} %x_ref.1, bf16[4,256,1024]{2,1,0:T(8,128)(2,1)} %c_ref.1, bf16[1024,512]{1,0:T(8,128)(2,1)S(1)} %copy-done, bf16[512,1024]{1,0:T(8,128)(2,1)S(1)} %copy-done.1), custom_call_target="tpu_custom_call" | custom-call | tf_op jit(solution)/shard_map/pallas_call | solution.py:270
  76.2 0.0 copy-done.3
  76.2 0.0 copy-start.4
  76.2 1.7 %convert_add_fusion.1 = f32[1024,512]{1,0:T(8,128)} fusion(f32[1024,512]{1,0:T(8,128)S(1)} %copy-done.3, bf16[1024,512]{1,0:T(8,128)(2,1)S(1)} %get-tuple-element.6), kind=kLoop, calls=%fused_computation.1 | loop fusion | flops 1048576 | bytes 5242880 | tf_op jit(solution)/shard_map/add | solution.py:301
  77.8 0.6 copy-done.4
  78.4 1.7 %convert_add_fusion = f32[512,1024]{1,0:T(8,128)} fusion(f32[512,1024]{1,0:T(8,128)S(1)} %copy-done.4, bf16[512,1024]{1,0:T(8,128)(2,1)S(1)} %get-tuple-element.7), kind=kLoop, calls=%fused_computation | loop fusion | flops 1048576 | bytes 5242880 | tf_op jit(solution)/shard_map/add | solution.py:302
  80.1 0.8 copy.11
Async XLA Ops:
  0.6 1.2 %copy-start = (bf16[1024,512]{1,0:T(8,128)(2,1)S(1)}, bf16[1024,512]{1,0:T(8,128)(2,1)}, u32[]{:S(2)}) copy-start(bf16[1024,512]{1,0:T(8,128)(2,1)} %wu_ref.1) | copy-start | bytes 3145732
  1.9 1.2 %copy-start.1 = (bf16[512,1024]{1,0:T(8,128)(2,1)S(1)}, bf16[512,1024]{1,0:T(8,128)(2,1)}, u32[]{:S(2)}) copy-start(bf16[512,1024]{1,0:T(8,128)(2,1)} %wd_ref.1) | copy-start | bytes 3145732
  3.1 0.7 copy-start.2
  3.7 72.4 %copy-start.3 = (f32[1024,512]{1,0:T(8,128)S(1)}, f32[1024,512]{1,0:T(8,128)}, u32[]{:S(2)}) copy-start(f32[1024,512]{1,0:T(8,128)} %param.12) | copy-start | bytes 6291460
  76.2 2.3 %copy-start.4 = (f32[512,1024]{1,0:T(8,128)S(1)}, f32[512,1024]{1,0:T(8,128)}, u32[]{:S(2)}) copy-start(f32[512,1024]{1,0:T(8,128)} %param.13) | copy-start | bytes 6291460
